TPU v7x, 32 devices: a whole 2x2x4 slice. The times are simulated.
32 devices in a mesh: grp: 2 (over x), gz: 16 (over z, y, core).
Axes of the slice: x: 2, y: 2, z: 4, core: 2. Of those that a mesh axis runs over, the one named last changes fastest.
Arguments:
- sections: bfloat16 [256, 512, 256], P(('grp', 'gz')), parts along dimension 0, may hold values from -40 to 40, as said below
- radius: int32 [2], replicated, may hold values from 2 to 16
Outputs:
- ncc_maps: bfloat16 [256, 8, 512, 256], P(('grp', 'gz')), parts along dimension 0
- positions: float32 [256], P(('grp', 'gz')), parts along dimension 0
There are 2 independent parts, one for each index of `grp`. A program takes and returns all parts, laid end to end along the dimension named above; an argument that names none is the same for every part. Nothing has to cross between parts.
Inputs may be any that keep to these rules, and one draw needn't show every extreme that they name: Rough from pixel to pixel; neighbouring sections are correlated.
All inputs are finite; a program needn't handle non-finite values.
Results may differ from a plain program's by a relative error of at most 0.0039.
Values may be sent and summed in bfloat16 or wider, within the bound.
A program may use at most 192 MiB of HBM per device.

v0:
```python
import jax
import jax.numpy as jnp
from jax import lax
from jax.sharding import PartitionSpec as P

TX = 512
TY = 256
REACH = 8


def from_behind(value, axis, steps):
    count = lax.axis_size(axis)
    first, last = (max(0, -steps), min(count, count - steps))
    return lax.ppermute(value, axis, [(source, source + steps) for source in range(first, last)])


def blur_table(count, radius_one):
    index = jnp.arange(count, dtype=jnp.int32)
    diff = index[:, None] - index[None, :]
    inside = jnp.abs(diff) <= radius_one
    sigma = radius_one.astype(jnp.float32) * 0.5
    dist = diff.astype(jnp.float32)
    table = jnp.where(inside, jnp.exp(-(dist * dist) / (2.0 * sigma * sigma)), jnp.float32(0.0))
    table = table / jnp.sum(table, axis=1, keepdims=True)
    return table.astype(jnp.bfloat16)


def blur_stack(stack, gx, gy):
    half = jnp.einsum("bik,jk->bij", stack, gy, preferred_element_type=jnp.float32).astype(
        jnp.bfloat16
    )
    return jnp.einsum("ij,bjk->bik", gx, half, preferred_element_type=jnp.float32)


def moments(stack, gx, gy):
    wide = stack.astype(jnp.float32)
    squares = (wide * wide).astype(jnp.bfloat16)
    count = stack.shape[0]
    both = blur_stack(jnp.concatenate([stack, squares], axis=0), gx, gy)
    return (both[:count], both[count:])


def pair_map(first, mu_a, var_a, partner, mu_b, sq_b, gx, gy):
    prod = (first.astype(jnp.float32) * partner.astype(jnp.float32)).astype(jnp.bfloat16)
    mixed = blur_stack(prod, gx, gy)
    var_b = sq_b - mu_b * mu_b
    return (mixed - mu_a * mu_b) / jnp.sqrt((var_a + 0.1) * (var_b + 0.1))


def per_device(sections, radius):
    gx = blur_table(TX, radius[0])
    gy = blur_table(TY, radius[1])
    count = sections.shape[0]
    mu_loc, sq_loc = moments(sections, gx, gy)
    var_a = sq_loc - mu_loc * mu_loc
    received = from_behind(sections, "gz", -1)
    mu_far, sq_far = moments(received, gx, gy)
    ext = jnp.concatenate([sections, received], axis=0)
    mu_ext = jnp.concatenate([mu_loc, mu_far], axis=0)
    sq_ext = jnp.concatenate([sq_loc, sq_far], axis=0)
    bands = []
    spacing = None
    for dist in range(1, REACH + 1):
        ncc = pair_map(
            sections,
            mu_loc,
            var_a,
            ext[dist : dist + count],
            mu_ext[dist : dist + count],
            sq_ext[dist : dist + count],
            gx,
            gy,
        )
        if dist == 1:
            spacing = 1.25 - jnp.mean(ncc, axis=(1, 2))
        bands.append(ncc.astype(jnp.bfloat16))
    ncc_maps = jnp.stack(bands, axis=1)
    running = jnp.cumsum(spacing)
    total = running[count - 1 : count]
    table = lax.all_gather(total, "gz", axis=0, tiled=True)
    earlier_runs = jnp.arange(table.shape[0], dtype=jnp.int32) < lax.axis_index("gz")
    before = jnp.sum(jnp.where(earlier_runs, table, jnp.float32(0.0)), keepdims=True)
    positions = (running + before) * 0.015625
    return (ncc_maps, positions)


def solution(mesh):
    in_specs = (P(("grp", "gz"), None, None), P())
    out_specs = (P(("grp", "gz"), None, None, None), P(("grp", "gz")))
    return jax.shard_map(
        per_device, mesh=mesh, in_specs=in_specs, out_specs=out_specs, check_vma=False
    )
```

profile of v0, /device:TPU:0, one launch (start us, length us, event | category | flops | bytes accessed | tf_op | source)
XLA Modules:
  0.0 208.5 jit_solution(16880154288525046987)
XLA Ops:
  0.6 0.0 copy-start
  0.6 1.4 collective-permute-start
  2.1 1.3 fusion.241
  4.8 1.3 dynamic-slice
  6.0 0.8 fusion.213
  6.8 1.2 fusion.192
  8.0 3.1 %constant_dynamic-update-slice_fusion.1 = bf16[16,512,256]{2,1,0:T(8,128)(2,1)} fusion(bf16[8,512,256]{2,1,0:T(8,128)(2,1)} %param.2), kind=kLoop, calls=%fused_computation.184 | loop fusion | bytes 4194304
  11.1 0.0 copy-done
  11.1 1.7 fusion.2
  12.7 9.8 %fusion.77 = f32[16,512,256]{1,2,0:T(8,128)} fusion(bf16[8,512,256]{2,1,0:T(8,128)(2,1)} %fusion.2, bf16[8,512,256]{2,1,0:T(8,128)(2,1)S(1)} %copy-done, f32[512]{0:T(512)S(1)} %fusion.192, f32[]{:T(128)S(6)} %mul.137, s32[]{:T(128)} %bitcast.2, f32[256]{0:T(256)S(1)} %fusion.213, f32[]{:T(128)S(6)} %mul.134, s32[]{:T(128)} %bitcast), kind=kOutput, calls=%fused_computation.122 | convolution fusion | flops 3228696576 | bytes 12586000 | tf_op jit(solution)/shard_map/ij,bjk->bik/dot_general | solution.py:32
  22.6 8.0 %fusion.240 = (f32[8,512,256]{1,2,0:T(8,128)}, f32[8,512,256]{1,2,0:T(8,128)}) fusion(f32[16,512,256]{1,2,0:T(8,128)} %fusion.77), kind=kLoop, calls=%fused_computation.203 | loop fusion | bytes 16777216 | tf_op jit(solution)/shard_map/slice | solution.py:40
  30.6 0.0 collective-permute-done
  30.6 3.3 %fusion = bf16[8,512,256]{2,1,0:T(8,128)(2,1)} fusion(bf16[8,512,256]{2,1,0:T(8,128)(2,1)} %collective-permute-done), kind=kLoop, calls=%fused_computation.34 | loop fusion | flops 3145728 | bytes 4194304 | tf_op jit(solution)/shard_map/convert_element_type | solution.py:37
  33.9 10.6 %fusion.80 = f32[16,512,256]{1,2,0:T(8,128)} fusion(bf16[8,512,256]{2,1,0:T(8,128)(2,1)} %fusion, bf16[8,512,256]{2,1,0:T(8,128)(2,1)} %collective-permute-done, f32[512]{0:T(512)S(1)} %fusion.192, f32[]{:T(128)S(6)} %mul.137, s32[]{:T(128)} %bitcast.2, f32[256]{0:T(256)S(1)} %fusion.213, f32[]{:T(128)S(6)} %mul.134, s32[]{:T(128)} %bitcast), kind=kOutput, calls=%fused_computation.123 | convolution fusion | flops 3228696576 | bytes 12586000 | tf_op jit(solution)/shard_map/ij,bjk->bik/dot_general | solution.py:32
  44.5 8.0 %fusion.239 = (f32[8,512,256]{1,2,0:T(8,128)}, f32[8,512,256]{1,2,0:T(8,128)}) fusion(f32[16,512,256]{1,2,0:T(8,128)} %fusion.80), kind=kLoop, calls=%fused_computation.202 | loop fusion | bytes 16777216 | tf_op jit(solution)/shard_map/slice | solution.py:40
  52.5 3.0 %constant_dynamic-update-slice_fusion = bf16[16,512,256]{2,1,0:T(8,128)(2,1)} fusion(bf16[16,512,256]{2,1,0:T(8,128)(2,1)} %constant_dynamic-update-slice_fusion.1, bf16[8,512,256]{2,1,0:T(8,128)(2,1)} %collective-permute-done), kind=kLoop, calls=%fused_computation.183 | loop fusion | bytes 4194304 | tf_op jit(solution)/shard_map/concatenate | solution.py:58
  55.6 11.6 %bitcast_dynamic-update-slice_fusion.7 = (bf16[8,8,512,256]{2,3,0,1:T(8,128)(2,1)}, f32[8,512,256]{1,2,0:T(8,128)}) fusion(f32[8,512,256]{1,2,0:T(8,128)} %get-tuple-element.7, f32[8,512,256]{1,2,0:T(8,128)} %get-tuple-element.9, f32[8,512,256]{1,2,0:T(8,128)} %get-tuple-element.8, f32[8,512,256]{1,2,0:T(8,128)} %get-tuple-element.6, f32[512]{0:T(512)S(1)} %fusion.192, ...), kind=kOutput, calls=%fused_computation.146 | convolution fusion | flops 1632763904 | bytes 27267080 | tf_op jit(solution)/shard_map/ij,bjk->bik/dot_general | solution.py:32
  67.2 10.6 %bitcast_dynamic-update-slice_fusion.6 = bf16[8,8,512,256]{2,3,0,1:T(8,128)(2,1)} fusion(bf16[8,8,512,256]{2,3,0,1:T(8,128)(2,1)} %get-tuple-element.12, f32[8,512,256]{1,2,0:T(8,128)} %get-tuple-element.7, f32[8,512,256]{1,2,0:T(8,128)} %get-tuple-element.9, f32[8,512,256]{1,2,0:T(8,128)} %get-tuple-element.8, f32[8,512,256]{1,2,0:T(8,128)} %get-tuple-element.6, ...), kind=kOutput, calls=%fused_computation.145 | convolution fusion | flops 1632763904 | bytes 23072776 | tf_op jit(solution)/shard_map/ij,bjk->bik/dot_general | solution.py:32
  77.8 10.7 %bitcast_dynamic-update-slice_fusion.5 = bf16[8,8,512,256]{2,3,0,1:T(8,128)(2,1)} fusion(bf16[8,8,512,256]{2,3,0,1:T(8,128)(2,1)} %bitcast_dynamic-update-slice_fusion.6, f32[8,512,256]{1,2,0:T(8,128)} %get-tuple-element.7, f32[8,512,256]{1,2,0:T(8,128)} %get-tuple-element.9, f32[8,512,256]{1,2,0:T(8,128)} %get-tuple-element.8, ...), kind=kOutput, calls=%fused_computation.144 | convolution fusion | flops 1632763904 | bytes 23072776 | tf_op jit(solution)/shard_map/ij,bjk->bik/dot_general | solution.py:32
  88.5 10.7 %bitcast_dynamic-update-slice_fusion.4 = bf16[8,8,512,256]{2,3,0,1:T(8,128)(2,1)} fusion(bf16[8,8,512,256]{2,3,0,1:T(8,128)(2,1)} %bitcast_dynamic-update-slice_fusion.5, f32[8,512,256]{1,2,0:T(8,128)} %get-tuple-element.7, f32[8,512,256]{1,2,0:T(8,128)} %get-tuple-element.9, f32[8,512,256]{1,2,0:T(8,128)} %get-tuple-element.8, ...), kind=kOutput, calls=%fused_computation.143 | convolution fusion | flops 1632763904 | bytes 23072776 | tf_op jit(solution)/shard_map/ij,bjk->bik/dot_general | solution.py:32
  99.2 10.7 %bitcast_dynamic-update-slice_fusion.3 = bf16[8,8,512,256]{2,3,0,1:T(8,128)(2,1)} fusion(bf16[8,8,512,256]{2,3,0,1:T(8,128)(2,1)} %bitcast_dynamic-update-slice_fusion.4, f32[8,512,256]{1,2,0:T(8,128)} %get-tuple-element.7, f32[8,512,256]{1,2,0:T(8,128)} %get-tuple-element.9, f32[8,512,256]{1,2,0:T(8,128)} %get-tuple-element.8, ...), kind=kOutput, calls=%fused_computation.142 | convolution fusion | flops 1632763904 | bytes 23072776 | tf_op jit(solution)/shard_map/ij,bjk->bik/dot_general | solution.py:32
  109.9 10.9 %bitcast_dynamic-update-slice_fusion.2 = bf16[8,8,512,256]{2,3,0,1:T(8,128)(2,1)} fusion(bf16[8,8,512,256]{2,3,0,1:T(8,128)(2,1)} %bitcast_dynamic-update-slice_fusion.3, f32[8,512,256]{1,2,0:T(8,128)} %get-tuple-element.7, f32[8,512,256]{1,2,0:T(8,128)} %get-tuple-element.9, f32[8,512,256]{1,2,0:T(8,128)} %get-tuple-element.8, ...), kind=kOutput, calls=%fused_computation.141 | convolution fusion | flops 1632763904 | bytes 23072776 | tf_op jit(solution)/shard_map/ij,bjk->bik/dot_general | solution.py:32
  120.8 10.7 %bitcast_dynamic-update-slice_fusion.1 = bf16[8,8,512,256]{2,3,0,1:T(8,128)(2,1)} fusion(bf16[8,8,512,256]{2,3,0,1:T(8,128)(2,1)} %bitcast_dynamic-update-slice_fusion.2, f32[8,512,256]{1,2,0:T(8,128)} %get-tuple-element.7, f32[8,512,256]{1,2,0:T(8,128)} %get-tuple-element.9, f32[8,512,256]{1,2,0:T(8,128)} %get-tuple-element.8, ...), kind=kOutput, calls=%fused_computation.140 | convolution fusion | flops 1632763904 | bytes 23072776 | tf_op jit(solution)/shard_map/ij,bjk->bik/dot_general | solution.py:32
  131.6 2.6 %reduce_sum.38 = f32[8]{0:T(128)S(1)} reduce(f32[8,512,256]{1,2,0:T(8,128)} %get-tuple-element.13, f32[]{:T(128)} %constant.8.clone.1), dimensions={1,2}, to_apply=%region_2.3 | reduce | flops 1048568 | bytes 4194340 | tf_op jit(solution)/shard_map/reduce_sum | solution.py:75
  134.1 0.2 reduce-window.4
  134.3 0.6 slice.114
  134.9 1.2 bitcast_dynamic-update-slice_fusion.8
  136.1 11.5 %bitcast_dynamic-update-slice_fusion = bf16[8,8,512,256]{2,3,0,1:T(8,128)(2,1)} fusion(bf16[8,8,512,256]{2,3,0,1:T(8,128)(2,1)} %bitcast_dynamic-update-slice_fusion.1, bf16[8,512,256]{2,1,0:T(8,128)(2,1)} %collective-permute-done, bf16[8,512,256]{2,1,0:T(8,128)(2,1)S(1)} %copy-done, f32[512]{0:T(512)S(1)} %fusion.192, f32[]{:T(128)S(6)} %mul.137, ...), kind=kOutput, calls=%fused_computation.139 | convolution fusion | flops 1630666752 | bytes 23072776 | tf_op jit(solution)/shard_map/ij,bjk->bik/dot_general | solution.py:32
  147.6 21.5 %copy.5 = bf16[8,8,512,256]{3,2,1,0:T(8,128)(2,1)} copy(bf16[8,8,512,256]{2,3,0,1:T(8,128)(2,1)} %bitcast_dynamic-update-slice_fusion) | data formatting | bytes 33554432
  169.1 37.5 %all-reduce = f32[16]{0:T(128)S(1)} all-reduce(f32[16]{0:T(128)S(1)} %bitcast_dynamic-update-slice_fusion.8), channel_id=2, replica_groups=mesh['grp'=2,'gz'=16] {'gz'}, use_global_device_ids=true, to_apply=%add | all-reduce | flops 16 | bytes 128 | tf_op jit(solution)/shard_map/all_gather | solution.py:80
  206.6 0.7 fusion.214
  207.3 1.2 multiply_bitcast_fusion
  (2 shorter events, 0.0 us)
Async XLA Ops:
  0.6 10.4 %copy-start = (bf16[8,512,256]{2,1,0:T(8,128)(2,1)S(1)}, bf16[8,512,256]{2,1,0:T(8,128)(2,1)}, u32[]{:S(2)}) copy-start(bf16[8,512,256]{2,1,0:T(8,128)(2,1)} %param.2) | copy-start | bytes 6291460
  0.6 30.0 %collective-permute-start = (bf16[8,512,256]{2,1,0:T(8,128)(2,1)}, bf16[8,512,256]{2,1,0:T(8,128)(2,1)}, u32[]{:S(2)}, u32[]{:S(2)}) collective-permute-start(bf16[8,512,256]{2,1,0:T(8,128)(2,1)} %param.2), channel_id=1, source_target_pairs={{1,0},{2,1},{3,2},{4,3},{5,4},{6,5},{7,6},{8,7},{9,8},{10,9},{11,1... | collective-permute-start | bytes 6291464 | tf_op jit(solution)/shard_map/ppermute | solution.py:14
where the time goes:
time: 210 us; the launch traced here: 209 us
  matrix products  108 us (51%)
  local copies, waits for them, and re-layouts  48.1 us (23%)
  blocking collectives  37.5 us (18%)
  other arithmetic  11.6 us (6%)
    dot_general x10, matrix products, blur_stack(): jnp.einsum('ij,bjk->bik', gx, half, preferred_element_type=jnp.float32)  108 us
    all_gather x1, blocking collectives, per_device(): table = lax.all_gather(total, 'gz', axis=0, tiled=True)  37.5 us
    unnamed x7, local copies, waits for them, and re-layouts  27.1 us
    slice x2, local copies, waits for them, and re-layouts, moments(): return (both[:count], both[count:])  16 us
    convert_element_type x2, other arithmetic, moments(): squares = (wide * wide).astype(jnp.bfloat16)  4.97 us
  transfers between devices with their start and end apart: 1, of which 0 were waited for; matrix products, arithmetic and copies ran while one was open for 13% of the time, Pallas kernels for 0%

commit v1 on v0

v1 whole, which is shorter than its diff:
```python
import functools

import jax
import jax.numpy as jnp
from jax import lax
from jax.experimental import pallas as pl
from jax.experimental.pallas import tpu as pltpu
from jax.sharding import PartitionSpec as P

REACH = 8
MAX_RADIUS = 16
ROWS = 176
BATCH = 2
VMEM_LIMIT = 20 * 2**20


def windows(tx):
    width = min(256, tx)
    out = []
    start = 0
    while start < tx:
        rows = min(ROWS, tx - start)
        middle = (start + rows // 2 - width // 2) // 16 * 16
        low = min(max(middle, 0), tx - width)
        assert low == 0 or low <= start - MAX_RADIUS
        assert low + width == tx or low + width >= start + rows + MAX_RADIUS
        out.append((start, rows, low))
        start += rows
    return width, out


def table(radius, shape, first, second, axis):
    i = lax.broadcasted_iota(jnp.int32, shape, 0) + first
    j = lax.broadcasted_iota(jnp.int32, shape, 1) + second
    diff = i - j
    sigma = radius.astype(jnp.float32) * 0.5
    dist = diff.astype(jnp.float32)
    value = jnp.exp(-(dist * dist) / (2.0 * sigma * sigma))
    value = jnp.where(jnp.abs(diff) <= radius, value, 0.0)
    return (value / jnp.sum(value, axis=axis, keepdims=True)).astype(jnp.bfloat16)


def blur_to(half_ref, gx_ref, blocks, width, slot, finish):
    for start, rows, low in blocks:
        acc = jnp.dot(
            gx_ref[start : start + rows, :],
            half_ref[slot, low : low + width, :],
            preferred_element_type=jnp.float32,
        )
        finish(start, rows, acc)


def fill_moments(src_ref, count, mu_ref, inv_ref, gx_ref, gy_ref, half_ref, blocks, width):
    def step(r, _):
        x = src_ref[r]
        half_ref[0] = jnp.dot(x, gy_ref[...], preferred_element_type=jnp.float32).astype(
            jnp.bfloat16
        )
        half_ref[1] = jnp.dot(x * x, gy_ref[...], preferred_element_type=jnp.float32).astype(
            jnp.bfloat16
        )
        for start, rows, low in blocks:
            gx = gx_ref[start : start + rows, :]
            mu = jnp.dot(
                gx, half_ref[0, low : low + width, :], preferred_element_type=jnp.float32
            )
            sq = jnp.dot(
                gx, half_ref[1, low : low + width, :], preferred_element_type=jnp.float32
            )
            mu_ref[r, start : start + rows, :] = mu
            inv_ref[r, start : start + rows, :] = lax.rsqrt(jnp.abs(sq - mu * mu + 0.1))
        return 0

    lax.fori_loop(0, count, step, 0)


def fill_pairs(
    runs, src_ref, far_ref, mu_a, inv_a, mu_b, inv_b, gx_ref, gy_ref,
    half_ref, stage, sems, sums_ref, ncc_ref, blocks, width, count,
):
    total = runs[-1][0] + runs[-1][4]
    steps = total // BATCH
    assert steps * BATCH == total and steps >= 2

    def decode(q):
        slot, place, s = jnp.int32(0), jnp.int32(0), jnp.int32(0)
        for first, run_slot, run_place, low, _ in runs:
            here = q >= first
            slot = jnp.where(here, run_slot, slot)
            place = jnp.where(here, run_place, place)
            s = jnp.where(here, low + q - first, s)
        return slot, s, place - s

    def copy(bank, b, s, d):
        return pltpu.make_async_copy(
            stage.at[bank * BATCH + b], ncc_ref.at[s, d - 1], sems.at[bank * BATCH + b]
        )

    def step(t, _):
        bank = lax.rem(t, 2)
        which = [decode(t * BATCH + b) for b in range(BATCH)]

        @pl.when(t >= 2)
        def _():
            for b in range(BATCH):
                copy(bank, b, 0, 1).wait()

        for b, (slot, s, d) in enumerate(which):
            half_ref[b] = jnp.dot(
                src_ref[s] * far_ref[slot], gy_ref[...], preferred_element_type=jnp.float32
            ).astype(jnp.bfloat16)
        for b, (slot, s, d) in enumerate(which):
            parts = []

            def finish(start, rows, acc):
                at = slice(start, start + rows)
                ncc = (acc - mu_a[s, at, :] * mu_b[slot, at, :]) * (
                    inv_a[s, at, :] * inv_b[slot, at, :]
                )
                stage[bank * BATCH + b, at, :] = ncc.astype(jnp.bfloat16)
                parts.append(jnp.sum(ncc.reshape(rows // 8, 8, ncc.shape[1]), axis=0))

            blur_to(half_ref, gx_ref, blocks, width, b, finish)
            sums_ref[jnp.where(d == 1, s, count)] = functools.reduce(jnp.add, parts)
            copy(bank, b, s, d).start()
        return 0

    lax.fori_loop(0, steps, step, 0)
    for bank in range(2):
        for b in range(BATCH):
            copy(bank, b, 0, 1).wait()


def local_kernel(
    blocks, width, runs, count,
    radius_ref, src_ref,
    ncc_ref, sums_ref, mu_ref, inv_ref, gx_ref, gy_ref,
    half_ref, stage, sems,
):
    for start, rows, low in blocks:
        gx_ref[start : start + rows, :] = table(radius_ref[0], (rows, width), start, low, 1)
    gy_ref[...] = table(radius_ref[1], gy_ref.shape, 0, 0, 0)
    fill_moments(src_ref, count, mu_ref, inv_ref, gx_ref, gy_ref, half_ref, blocks, width)
    fill_pairs(
        runs, src_ref, src_ref, mu_ref, inv_ref, mu_ref, inv_ref, gx_ref, gy_ref,
        half_ref, stage, sems, sums_ref, ncc_ref, blocks, width, count,
    )


def far_kernel(
    blocks, width, runs, count,
    src_ref, far_ref, mu_ref, inv_ref, gx_ref, gy_ref, old_ref,
    ncc_ref, sums_ref,
    mu_far, inv_far, half_ref, stage, sems,
):
    fill_moments(
        far_ref, far_ref.shape[0], mu_far, inv_far, gx_ref, gy_ref, half_ref, blocks, width
    )
    fill_pairs(
        runs, src_ref, far_ref, mu_ref, inv_ref, mu_far, inv_far, gx_ref, gy_ref,
        half_ref, stage, sems, sums_ref, ncc_ref, blocks, width, count,
    )


def make_runs(places, count):
    out = []
    first = 0
    for slot, place in places:
        low, high = max(0, place - REACH), min(place, count)
        if high > low:
            out.append((first, slot, place, low, high - low))
            first += high - low
    return out


def per_device(sections, radius):
    count, tx, ty = sections.shape
    width, blocks = windows(tx)
    axis = lax.axis_size("gz")
    back = [(i, i - 1) for i in range(1, axis)]
    cuts = [0, 1, 4, REACH]
    received = [
        lax.ppermute(sections[a:b], "gz", back) for a, b in zip(cuts[:-1], cuts[1:])
    ]
    vmem = pl.BlockSpec(memory_space=pltpu.VMEM)
    smem = pl.BlockSpec(memory_space=pltpu.SMEM)
    hbm = pl.BlockSpec(memory_space=pl.ANY)
    shape = jax.ShapeDtypeStruct
    ncc_type = shape((count, REACH, tx, ty), jnp.bfloat16)
    sums_type = shape((count + 1, 8, ty), jnp.float32)
    map_type = shape((count, tx, ty), jnp.float32)
    work = [
        pltpu.VMEM((2, tx, ty), jnp.bfloat16),
        pltpu.VMEM((2 * BATCH, tx, ty), jnp.bfloat16),
        pltpu.SemaphoreType.DMA((2 * BATCH,)),
    ]
    params = pltpu.CompilerParams(vmem_limit_bytes=VMEM_LIMIT)

    def cost(maps):
        return pl.CostEstimate(
            flops=maps * 2 * tx * ty * (ty + width),
            bytes_accessed=maps * tx * ty * 2,
            transcendentals=0,
        )

    runs = make_runs([(p, p) for p in range(count)], count)
    ncc, sums, mu, inv, gx, gy = pl.pallas_call(
        functools.partial(local_kernel, blocks, width, runs, count),
        out_shape=(
            ncc_type, sums_type, map_type, map_type,
            shape((tx, width), jnp.bfloat16), shape((ty, ty), jnp.bfloat16),
        ),
        in_specs=[smem, vmem],
        out_specs=(hbm, vmem, vmem, vmem, vmem, vmem),
        scratch_shapes=work,
        compiler_params=params,
        cost_estimate=cost(44),
        name="local_pairs",
    )(radius, sections)
    near = jnp.sum(sums[: count - 1], axis=(1, 2))
    positions = None
    for k, (a, b) in enumerate(zip(cuts[:-1], cuts[1:])):
        runs = make_runs([(j - a, count + j) for j in range(a, b)], count)
        ncc, sums = pl.pallas_call(
            functools.partial(far_kernel, blocks, width, runs, count),
            out_shape=(ncc_type, sums_type),
            in_specs=[vmem] * 6 + [hbm],
            out_specs=(hbm, vmem),
            scratch_shapes=[pltpu.VMEM((b - a, tx, ty), jnp.float32)] * 2 + work,
            input_output_aliases={6: 0},
            compiler_params=params,
            cost_estimate=cost(sum(r[4] for r in runs) + 2 * (b - a)),
            name=f"far_pairs_{k}",
        )(sections, received[k], mu, inv, gx, gy, ncc)
        if k == 0:
            last = jnp.sum(sums[count - 1 : count], axis=(1, 2))
            spacing = 1.25 - jnp.concatenate([near, last]) / (tx * ty)
            every = lax.all_gather(jnp.sum(spacing, keepdims=True), "gz", axis=0, tiled=True)
            earlier = jnp.arange(axis, dtype=jnp.int32) < lax.axis_index("gz")
            before = jnp.sum(jnp.where(earlier, every, 0.0))
            order = jnp.arange(count, dtype=jnp.int32)
            running = jnp.sum(
                jnp.where(order[None, :] <= order[:, None], spacing[None, :], 0.0), axis=1
            )
            positions = (running + before) * 0.015625
    return (ncc, positions)


def solution(mesh):
    in_specs = (P(("grp", "gz"), None, None), P())
    out_specs = (P(("grp", "gz"), None, None, None), P(("grp", "gz")))
    return jax.shard_map(
        per_device, mesh=mesh, in_specs=in_specs, out_specs=out_specs, check_vma=False
    )
```

time: 210 us -> 108 us (0.51)
  matrix products: 108 us -> 0 us
  Pallas kernels: 0 us -> 36.1 us
  local copies, waits for them, and re-layouts: 48.1 us -> 23.8 us
  other arithmetic: 11.6 us -> 4.91 us
  starting transfers between devices: 1.42 us -> 3.84 us
    dot_general x10 -> x0, matrix products: 108 us -> none  [blur_stack(): jnp.einsum('ij,bjk->bik', gx, half, preferred_element_type=jnp.float32)]
    unnamed x0 -> x1, blocking collectives: none -> 38.1 us
    all_gather x1 -> x0, blocking collectives: 37.5 us -> none  [per_device(): table = lax.all_gather(total, 'gz', axis=0, tiled=True)]
    pallas_call x0 -> x4, Pallas kernels: none -> 36.1 us  [the longest x3 21.3 us: per_device(): pl.pallas_call(functools.partial(far_kernel, blocks, width, runs, count),...]
    slice x4 -> x3, local copies, waits for them, and re-layouts: 17.9 us -> 6.28 us  [per_device(): sections[a:b]]
    unnamed x7 -> x25, local copies, waits for them, and re-layouts: 27.1 us -> 17.5 us
    convert_element_type x2 -> x0, other arithmetic: 4.97 us -> none  [moments(): squares = (wide * wide).astype(jnp.bfloat16)]
    concatenate x1 -> x0, local copies, waits for them, and re-layouts: 3.04 us -> none  [per_device(): ext = jnp.concatenate([sections, received], axis=0)]
  transfers between devices with their start and end apart: 1 -> 3, of which waited for: 0 -> 0; matrix products, arithmetic and copies ran while one was open for 13% -> 11% of each run, Pallas kernels for 0% -> 27%
where the time goes in v1:
time: 108 us
  blocking collectives  38.1 us (35%)
  Pallas kernels  36.1 us (33%)
  local copies, waits for them, and re-layouts  23.8 us (22%)
  other arithmetic  4.91 us (5%)
  starting transfers between devices  3.84 us (4%)
    unnamed x1, blocking collectives  38.1 us
    pallas_call x3, Pallas kernels, per_device(): pl.pallas_call(functools.partial(far_kernel, blocks, width, runs, count),...  21.3 us
    unnamed x25, local copies, waits for them, and re-layouts  17.5 us
    pallas_call x1, Pallas kernels, per_device(): pl.pallas_call(functools.partial(local_kernel, blocks, width, runs, count...  14.8 us
    slice x3, local copies, waits for them, and re-layouts, per_device(): sections[a:b]  6.28 us
    ppermute x3, starting transfers between devices, per_device(): lax.ppermute(sections[a:b], 'gz', back)  3.84 us
  transfers between devices with their start and end apart: 3, of which 0 were waited for; matrix products, arithmetic and copies ran while one was open for 11% of the time, Pallas kernels for 27%

profile of v1, /device:TPU:0, one launch (start us, length us, event | category | flops | bytes accessed | tf_op | source)
XLA Modules:
  0.0 107.5 jit_solution(17202057688890318711)
XLA Ops:
  0.6 0.0 copy-start.10
  0.6 0.0 copy-start.7
  0.7 1.8 %slice.17 = bf16[1,512,256]{2,1,0:T(8,128)(2,1)} slice(bf16[8,512,256]{2,1,0:T(8,128)(2,1)} %src_ref.7), slice={[0:1], [0:512], [0:256]} | slice | bytes 524288 | tf_op jit(solution)/shard_map/slice | solution.py:183
  2.5 1.3 %collective-permute-start.2 = (bf16[1,512,256]{2,1,0:T(8,128)(2,1)}, bf16[1,512,256]{2,1,0:T(8,128)(2,1)}, u32[]{:S(2)}, u32[]{:S(2)}) collective-permute-start(bf16[1,512,256]{2,1,0:T(8,128)(2,1)} %slice.17), channel_id=1, source_target_pairs={{1,0},{2,1},{3,2},{4,3},{5,4},{6,5},{7,6},{8,7},{9,8},{10,9},{11,1... | collective-permute-start | bytes 786440 | tf_op jit(solution)/shard_map/ppermute | solution.py:183
  3.8 2.1 %slice.16 = bf16[3,512,256]{2,1,0:T(8,128)(2,1)} slice(bf16[8,512,256]{2,1,0:T(8,128)(2,1)} %src_ref.7), slice={[1:4], [0:512], [0:256]} | slice | bytes 1572864 | tf_op jit(solution)/shard_map/slice | solution.py:183
  5.9 1.3 %collective-permute-start.1 = (bf16[3,512,256]{2,1,0:T(8,128)(2,1)}, bf16[3,512,256]{2,1,0:T(8,128)(2,1)}, u32[]{:S(2)}, u32[]{:S(2)}) collective-permute-start(bf16[3,512,256]{2,1,0:T(8,128)(2,1)} %slice.16), channel_id=1, source_target_pairs={{1,0},{2,1},{3,2},{4,3},{5,4},{6,5},{7,6},{8,7},{9,8},{10,9},{11,1... | collective-permute-start | bytes 2359304 | tf_op jit(solution)/shard_map/ppermute | solution.py:183
  7.2 2.3 %slice.15 = bf16[4,512,256]{2,1,0:T(8,128)(2,1)} slice(bf16[8,512,256]{2,1,0:T(8,128)(2,1)} %src_ref.7), slice={[4:8], [0:512], [0:256]} | slice | bytes 2097152 | tf_op jit(solution)/shard_map/slice | solution.py:183
  9.5 1.3 %collective-permute-start = (bf16[4,512,256]{2,1,0:T(8,128)(2,1)}, bf16[4,512,256]{2,1,0:T(8,128)(2,1)S(1)}, u32[]{:S(2)}, u32[]{:S(2)}) collective-permute-start(bf16[4,512,256]{2,1,0:T(8,128)(2,1)} %slice.15), channel_id=1, source_target_pairs={{1,0},{2,1},{3,2},{4,3},{5,4},{6,5},{7,6},{8,7},{9,8},{10,9},{11,1... | collective-permute-start | bytes 3145736 | tf_op jit(solution)/shard_map/ppermute | solution.py:183
  10.8 0.0 copy-start.6
  10.8 1.6 %copy-done.6 = bf16[8,512,256]{2,1,0:T(8,128)(2,1)S(1)} copy-done((bf16[8,512,256]{2,1,0:T(8,128)(2,1)S(1)}, bf16[8,512,256]{2,1,0:T(8,128)(2,1)}, u32[]{:S(2)}) %copy-start.6) | copy-done | bytes 2097176
  12.4 0.0 copy-start.9
  12.4 0.7 copy-done.9
  13.0 14.8 %local_pairs.1 = (bf16[8,8,512,256]{3,2,1,0:T(8,128)(2,1)}, f32[9,8,256]{2,1,0:T(8,128)S(1)}, f32[8,512,256]{2,1,0:T(8,128)S(1)}, f32[8,512,256]{2,1,0:T(8,128)S...) custom-call(s32[2]{0:T(128)S(1)} %copy-done.9, bf16[8,512,256]{2,1,0:T(8,128)(2,1)S(1)} %copy-done.6), custom_call_target="tpu_custom_call" | custom-call | flops 5905580032 | bytes 11534336 | tf_op jit(solution)/shard_map/local_pairs/pallas_call | solution.py:207
  27.9 0.0 copy-start
  27.9 1.9 %copy-done = f32[8,512,256]{2,1,0:T(8,128)} copy-done((f32[8,512,256]{2,1,0:T(8,128)}, f32[8,512,256]{2,1,0:T(8,128)S(1)}, u32[]{:S(2)}) %copy-start) | copy-done | bytes 4194328
  29.8 0.0 copy-start.3
  29.8 2.0 %copy-done.3 = f32[8,512,256]{2,1,0:T(8,128)} copy-done((f32[8,512,256]{2,1,0:T(8,128)}, f32[8,512,256]{2,1,0:T(8,128)S(1)}, u32[]{:S(2)}) %copy-start.3) | copy-done | bytes 4194328
  31.8 0.0 copy-start.8
  31.8 0.6 copy-done.8
  32.4 0.0 copy-done.10
  32.4 0.6 dynamic-slice
  33.0 1.0 slice_reduce_fusion
  34.0 0.0 collective-permute-done.2.far_ref
  34.0 0.0 copy-done.7
  34.0 0.0 copy-start.1
  34.0 2.2 %copy-done.1 = f32[8,512,256]{2,1,0:T(8,128)S(1)} copy-done((f32[8,512,256]{2,1,0:T(8,128)S(1)}, f32[8,512,256]{2,1,0:T(8,128)}, u32[]{:S(2)}) %copy-start.1) | copy-done | bytes 4194328
  36.2 0.0 copy-start.4
  36.2 2.2 %copy-done.4 = f32[8,512,256]{2,1,0:T(8,128)S(1)} copy-done((f32[8,512,256]{2,1,0:T(8,128)S(1)}, f32[8,512,256]{2,1,0:T(8,128)}, u32[]{:S(2)}) %copy-start.4) | copy-done | bytes 4194328
  38.4 4.7 %far_pairs_0.1 = (bf16[8,8,512,256]{3,2,1,0:T(8,128)(2,1)}, f32[9,8,256]{2,1,0:T(8,128)S(1)}) custom-call(bf16[8,512,256]{2,1,0:T(8,128)(2,1)S(1)} %copy-done.7, bf16[1,512,256]{2,1,0:T(8,128)(2,1)} %collective-permute-done.2.far_ref, f32[8,512,256]{2,1,0:T(8,128)S(1)} %copy-done.1, f32[8,512,256]{2,1,0:T(8,128)S(1)} %copy-done.4, ...), custom_call_target="tpu_custom_call", output_to_operand_aliasing={{0}: (6, {})} | custom-call | flops 1342177280 | bytes 2621440 | tf_op jit(solution)/shard_map/far_pairs_0/pallas_call | solution.py:224
  43.1 0.6 slice_reduce_fusion.1
  43.7 1.4 %fusion.2 = (f32[]{:T(128)}, f32[8]{0:T(128)S(1)}) fusion(f32[1]{0:T(128)} %bitcast, f32[7]{0:T(128)S(1)} %slice_reduce_fusion), kind=kLoop, calls=%fused_computation.9 | loop fusion | flops 31 | bytes 68 | tf_op jit(solution)/shard_map/reduce_sum | solution.py:238
  45.1 1.4 %dynamic-update-slice = f32[16]{0:T(128)S(1)} dynamic-update-slice(f32[16]{0:T(128)S(1)} %broadcast.21, f32[1]{0:T(128)} %bitcast.1, u32[]{:T(128)} %bitcast.2) | dynamic-update-slice | bytes 12
  46.5 38.1 %all-reduce = f32[16]{0:T(128)S(1)} all-reduce(f32[16]{0:T(128)S(1)} %dynamic-update-slice), channel_id=1, replica_groups=mesh['grp'=2,'gz'=16] {'gz'}, use_global_device_ids=true, to_apply=%add | all-reduce | flops 16 | bytes 128
  84.6 0.1 select_reduce_fusion
  84.7 0.7 fusion
  85.4 1.2 %add_multiply_fusion = f32[8]{0:T(128)} fusion(f32[8]{0:T(128)S(1)} %select_reduce_fusion, f32[]{:T(128)} %fusion), kind=kLoop, calls=%fused_computation.8 | loop fusion | flops 16 | bytes 68 | tf_op jit(solution)/shard_map/mul | solution.py:245
  86.5 0.0 collective-permute-done.1.far_ref
  86.5 0.0 copy-start.2
  86.6 2.2 %copy-done.2 = f32[8,512,256]{2,1,0:T(8,128)S(1)} copy-done((f32[8,512,256]{2,1,0:T(8,128)S(1)}, f32[8,512,256]{2,1,0:T(8,128)}, u32[]{:S(2)}) %copy-start.2) | copy-done | bytes 4194328
  88.7 0.0 copy-start.5
  88.7 2.2 %copy-done.5 = f32[8,512,256]{2,1,0:T(8,128)S(1)} copy-done((f32[8,512,256]{2,1,0:T(8,128)S(1)}, f32[8,512,256]{2,1,0:T(8,128)}, u32[]{:S(2)}) %copy-start.5) | copy-done | bytes 4194328
  90.9 9.9 %far_pairs_1.1 = (bf16[8,8,512,256]{3,2,1,0:T(8,128)(2,1)}, f32[9,8,256]{2,1,0:T(8,128)}) custom-call(bf16[8,512,256]{2,1,0:T(8,128)(2,1)S(1)} %copy-done.7, bf16[3,512,256]{2,1,0:T(8,128)(2,1)} %collective-permute-done.1.far_ref, f32[8,512,256]{2,1,0:T(8,128)S(1)} %copy-done.2, f32[8,512,256]{2,1,0:T(8,128)S(1)} %copy-done.5, ...), custom_call_target="tpu_custom_call", output_to_operand_aliasing={{0}: (6, {})} | custom-call | flops 3221225472 | bytes 6291456 | tf_op jit(solution)/shard_map/far_pairs_1/pallas_call | solution.py:224
  100.8 0.0 collective-permute-done.far_ref
  100.8 6.7 %far_pairs_2.1 = (bf16[8,8,512,256]{3,2,1,0:T(8,128)(2,1)}, f32[9,8,256]{2,1,0:T(8,128)}) custom-call(bf16[8,512,256]{2,1,0:T(8,128)(2,1)S(1)} %copy-done.7, bf16[4,512,256]{2,1,0:T(8,128)(2,1)S(1)} %collective-permute-done.far_ref, f32[8,512,256]{2,1,0:T(8,128)S(1)} %copy-done.2, f32[8,512,256]{2,1,0:T(8,128)S(1)} %copy-done.5, ...), custom_call_target="tpu_custom_call", output_to_operand_aliasing={{0}: (6, {})} | custom-call | flops 2415919104 | bytes 4718592 | tf_op jit(solution)/shard_map/far_pairs_2/pallas_call | solution.py:224
  (1 shorter events, 0.0 us)
Async XLA Ops:
  0.6 31.8 %copy-start.10 = (u32[32]{0:T(128)S(1)}, u32[32]{0:T(128)}, u32[]{:S(2)}) copy-start(u32[32]{0:T(128)} %constant.16) | copy-start | bytes 388
  0.6 33.3 %copy-start.7 = (bf16[8,512,256]{2,1,0:T(8,128)(2,1)S(1)}, bf16[8,512,256]{2,1,0:T(8,128)(2,1)}, u32[]{:S(2)}) copy-start(bf16[8,512,256]{2,1,0:T(8,128)(2,1)} %src_ref.7) | copy-start | bytes 6291460
  2.5 31.5 %collective-permute-start.2 = (bf16[1,512,256]{2,1,0:T(8,128)(2,1)}, bf16[1,512,256]{2,1,0:T(8,128)(2,1)}, u32[]{:S(2)}, u32[]{:S(2)}) collective-permute-start(bf16[1,512,256]{2,1,0:T(8,128)(2,1)} %slice.17), channel_id=1, source_target_pairs={{1,0},{2,1},{3,2},{4,3},{5,4},{6,5},{7,6},{8,7},{9,8},{10,9},{11,1... | collective-permute-start | bytes 786440 | tf_op jit(solution)/shard_map/ppermute | solution.py:183
  5.9 80.7 %collective-permute-start.1 = (bf16[3,512,256]{2,1,0:T(8,128)(2,1)}, bf16[3,512,256]{2,1,0:T(8,128)(2,1)}, u32[]{:S(2)}, u32[]{:S(2)}) collective-permute-start(bf16[3,512,256]{2,1,0:T(8,128)(2,1)} %slice.16), channel_id=1, source_target_pairs={{1,0},{2,1},{3,2},{4,3},{5,4},{6,5},{7,6},{8,7},{9,8},{10,9},{11,1... | collective-permute-start | bytes 2359304 | tf_op jit(solution)/shard_map/ppermute | solution.py:183
  9.5 91.3 %collective-permute-start = (bf16[4,512,256]{2,1,0:T(8,128)(2,1)}, bf16[4,512,256]{2,1,0:T(8,128)(2,1)S(1)}, u32[]{:S(2)}, u32[]{:S(2)}) collective-permute-start(bf16[4,512,256]{2,1,0:T(8,128)(2,1)} %slice.15), channel_id=1, source_target_pairs={{1,0},{2,1},{3,2},{4,3},{5,4},{6,5},{7,6},{8,7},{9,8},{10,9},{11,1... | collective-permute-start | bytes 3145736 | tf_op jit(solution)/shard_map/ppermute | solution.py:183
  10.8 1.6 %copy-start.6 = (bf16[8,512,256]{2,1,0:T(8,128)(2,1)S(1)}, bf16[8,512,256]{2,1,0:T(8,128)(2,1)}, u32[]{:S(2)}) copy-start(bf16[8,512,256]{2,1,0:T(8,128)(2,1)} %src_ref.7) | copy-start | bytes 6291460
  12.4 0.7 copy-start.9
  27.9 1.9 %copy-start = (f32[8,512,256]{2,1,0:T(8,128)}, f32[8,512,256]{2,1,0:T(8,128)S(1)}, u32[]{:S(2)}) copy-start(f32[8,512,256]{2,1,0:T(8,128)S(1)} %get-tuple-element.12.mu_ref) | copy-start | bytes 12582916
  29.8 2.0 %copy-start.3 = (f32[8,512,256]{2,1,0:T(8,128)}, f32[8,512,256]{2,1,0:T(8,128)S(1)}, u32[]{:S(2)}) copy-start(f32[8,512,256]{2,1,0:T(8,128)S(1)} %get-tuple-element.13.inv_ref) | copy-start | bytes 12582916
  31.8 0.6 copy-start.8
  34.0 2.2 %copy-start.1 = (f32[8,512,256]{2,1,0:T(8,128)S(1)}, f32[8,512,256]{2,1,0:T(8,128)}, u32[]{:S(2)}) copy-start(f32[8,512,256]{2,1,0:T(8,128)} %copy-done) | copy-start | bytes 12582916
  36.2 2.2 %copy-start.4 = (f32[8,512,256]{2,1,0:T(8,128)S(1)}, f32[8,512,256]{2,1,0:T(8,128)}, u32[]{:S(2)}) copy-start(f32[8,512,256]{2,1,0:T(8,128)} %copy-done.3) | copy-start | bytes 12582916
  86.5 2.2 %copy-start.2 = (f32[8,512,256]{2,1,0:T(8,128)S(1)}, f32[8,512,256]{2,1,0:T(8,128)}, u32[]{:S(2)}) copy-start(f32[8,512,256]{2,1,0:T(8,128)} %copy-done) | copy-start | bytes 12582916
  88.7 2.2 %copy-start.5 = (f32[8,512,256]{2,1,0:T(8,128)S(1)}, f32[8,512,256]{2,1,0:T(8,128)}, u32[]{:S(2)}) copy-start(f32[8,512,256]{2,1,0:T(8,128)} %copy-done.3) | copy-start | bytes 12582916

commit v2 on v1

--- a/solution.py
+++ b/solution.py
@@ -9,9 +9,10 @@
 
 REACH = 8
 MAX_RADIUS = 16
+LANES = 128
 ROWS = 176
 BATCH = 2
-VMEM_LIMIT = 20 * 2**20
+VMEM_LIMIT = 26 * 2**20
 
 
 def windows(tx):
@@ -162,6 +163,44 @@
     )
 
 
+def share_kernel(
+    devices, count, pixels, near_ref, far_ref, out_ref, mine, slots, send_sems, recv_sems
+):
+    me = lax.axis_index("gz")
+    barrier = pltpu.get_barrier_semaphore()
+    peers = [lax.rem(me + k, devices) for k in range(1, devices)]
+    for peer in peers:
+        pl.semaphore_signal(
+            barrier, inc=1, device_id={"gz": peer}, device_id_type=pl.DeviceIdType.MESH
+        )
+    near = jnp.sum(jnp.sum(near_ref[:count], axis=1), axis=1, keepdims=True)
+    last = jnp.sum(jnp.sum(far_ref[count - 1 : count], axis=1), axis=1, keepdims=True)
+    row = lax.broadcasted_iota(jnp.int32, (count, LANES), 0)
+    lane = lax.broadcasted_iota(jnp.int32, (count, LANES), 1)
+    sums = jnp.where(row < count - 1, near, last)
+    spacing = 1.25 - sums / pixels
+    mine[...] = jnp.broadcast_to(jnp.sum(spacing, axis=0, keepdims=True), mine.shape)
+    running = jnp.sum(jnp.where(row <= lane, spacing, 0.0), axis=0, keepdims=True)
+    pl.semaphore_wait(barrier, devices - 1)
+    copies = []
+    for k, peer in enumerate(peers, 1):
+        copy = pltpu.make_async_remote_copy(
+            src_ref=mine,
+            dst_ref=slots.at[k],
+            send_sem=send_sems.at[k],
+            recv_sem=recv_sems.at[k],
+            device_id={"gz": peer},
+            device_id_type=pl.DeviceIdType.MESH,
+        )
+        copy.start()
+        copies.append(copy)
+    for copy in copies:
+        copy.wait()
+    for k in range(1, devices):
+        running = running + jnp.where(k <= me, slots[k, :1, :], 0.0)
+    out_ref[...] = running * 0.015625
+
+
 def make_runs(places, count):
     out = []
     first = 0
@@ -178,10 +217,7 @@
     width, blocks = windows(tx)
     axis = lax.axis_size("gz")
     back = [(i, i - 1) for i in range(1, axis)]
-    cuts = [0, 1, 4, REACH]
-    received = [
-        lax.ppermute(sections[a:b], "gz", back) for a, b in zip(cuts[:-1], cuts[1:])
-    ]
+    received = lax.ppermute(sections, "gz", back)
     vmem = pl.BlockSpec(memory_space=pltpu.VMEM)
     smem = pl.BlockSpec(memory_space=pltpu.SMEM)
     hbm = pl.BlockSpec(memory_space=pl.ANY)
@@ -217,33 +253,33 @@
         cost_estimate=cost(44),
         name="local_pairs",
     )(radius, sections)
-    near = jnp.sum(sums[: count - 1], axis=(1, 2))
-    positions = None
-    for k, (a, b) in enumerate(zip(cuts[:-1], cuts[1:])):
-        runs = make_runs([(j - a, count + j) for j in range(a, b)], count)
-        ncc, sums = pl.pallas_call(
-            functools.partial(far_kernel, blocks, width, runs, count),
-            out_shape=(ncc_type, sums_type),
-            in_specs=[vmem] * 6 + [hbm],
-            out_specs=(hbm, vmem),
-            scratch_shapes=[pltpu.VMEM((b - a, tx, ty), jnp.float32)] * 2 + work,
-            input_output_aliases={6: 0},
-            compiler_params=params,
-            cost_estimate=cost(sum(r[4] for r in runs) + 2 * (b - a)),
-            name=f"far_pairs_{k}",
-        )(sections, received[k], mu, inv, gx, gy, ncc)
-        if k == 0:
-            last = jnp.sum(sums[count - 1 : count], axis=(1, 2))
-            spacing = 1.25 - jnp.concatenate([near, last]) / (tx * ty)
-            every = lax.all_gather(jnp.sum(spacing, keepdims=True), "gz", axis=0, tiled=True)
-            earlier = jnp.arange(axis, dtype=jnp.int32) < lax.axis_index("gz")
-            before = jnp.sum(jnp.where(earlier, every, 0.0))
-            order = jnp.arange(count, dtype=jnp.int32)
-            running = jnp.sum(
-                jnp.where(order[None, :] <= order[:, None], spacing[None, :], 0.0), axis=1
-            )
-            positions = (running + before) * 0.015625
-    return (ncc, positions)
+    runs = make_runs([(j, count + j) for j in range(REACH)], count)
+    ncc, sums_far = pl.pallas_call(
+        functools.partial(far_kernel, blocks, width, runs, count),
+        out_shape=(ncc_type, sums_type),
+        in_specs=[vmem] * 6 + [hbm],
+        out_specs=(hbm, vmem),
+        scratch_shapes=[pltpu.VMEM((REACH, tx, ty), jnp.float32)] * 2 + work,
+        input_output_aliases={6: 0},
+        compiler_params=params,
+        cost_estimate=cost(52),
+        name="far_pairs",
+    )(sections, received, mu, inv, gx, gy, ncc)
+    positions = pl.pallas_call(
+        functools.partial(share_kernel, axis, count, tx * ty),
+        out_shape=shape((1, LANES), jnp.float32),
+        in_specs=[vmem] * 2,
+        out_specs=vmem,
+        scratch_shapes=[
+            pltpu.VMEM((8, LANES), jnp.float32),
+            pltpu.VMEM((axis, 8, LANES), jnp.float32),
+            pltpu.SemaphoreType.DMA((axis,)),
+            pltpu.SemaphoreType.DMA((axis,)),
+        ],
+        compiler_params=pltpu.CompilerParams(collective_id=0, has_side_effects=True),
+        name="share_totals",
+    )(sums, sums_far)
+    return (ncc, positions[0, :count])
 
 
 def solution(mesh):

time: 108 us -> 58.6 us (0.54)
  blocking collectives: 38.1 us -> 0 us
  local copies, waits for them, and re-layouts: 23.8 us -> 3.99 us
  Pallas kernels: 36.1 us -> 52.4 us
  other arithmetic: 4.91 us -> 0 us
  starting transfers between devices: 3.84 us -> 1.29 us
    unnamed x1 -> x0, blocking collectives: 38.1 us -> none
    pallas_call x0 -> x1, Pallas kernels: none -> 19.1 us  [per_device(): pl.pallas_call(functools.partial(share_kernel, axis, count, tx * ty), out...]
    unnamed x25 -> x8, local copies, waits for them, and re-layouts: 17.5 us -> 2.86 us
    slice x3 -> x0, local copies, waits for them, and re-layouts: 6.28 us -> none  [per_device(): sections[a:b]]
    reduce_sum x5 -> x0, other arithmetic: 3.72 us -> none  [the longest x1 1.38 us: per_device(): jnp.sum(spacing, keepdims=True)]
    pallas_call x3 -> x1, Pallas kernels: 21.3 us -> 18.2 us  [per_device(): pl.pallas_call(functools.partial(far_kernel, blocks, width, runs, count),...]
    ppermute x3 -> x1, starting transfers between devices: 3.84 us -> 1.29 us  [per_device(): received = lax.ppermute(sections, 'gz', back)]
    mul x1 -> x0, other arithmetic: 1.19 us -> none  [per_device(): positions = (running + before) * 0.015625]
  transfers between devices with their start and end apart: 3 -> 1, of which waited for: 0 -> 0; matrix products, arithmetic and copies ran while one was open for 11% -> 0% of each run, Pallas kernels for 27% -> 26%
where the time goes in v2:
time: 58.6 us; the launch traced here: 58.4 us
  Pallas kernels  52.4 us (89%)
  local copies, waits for them, and re-layouts  3.99 us (7%)
  starting transfers between devices  1.29 us (2%)
  between operations  0.7 us (1%)
    pallas_call x1, Pallas kernels, per_device(): pl.pallas_call(functools.partial(share_kernel, axis, count, tx * ty), out...  19.1 us
    pallas_call x1, Pallas kernels, per_device(): pl.pallas_call(functools.partial(far_kernel, blocks, width, runs, count),...  18.2 us
    pallas_call x1, Pallas kernels, per_device(): pl.pallas_call(functools.partial(local_kernel, blocks, width, runs, count...  15 us
    unnamed x8, local copies, waits for them, and re-layouts  2.86 us
    ppermute x1, starting transfers between devices, per_device(): received = lax.ppermute(sections, 'gz', back)  1.29 us
  transfers between devices with their start and end apart: 1, of which 0 were waited for; matrix products, arithmetic and copies ran while one was open for 0% of the time, Pallas kernels for 26%

profile of v2, /device:TPU:0, one launch (start us, length us, event | category | flops | bytes accessed | tf_op | source)
XLA Modules:
  0.0 58.4 jit_solution(1507079132416528726)
XLA Ops:
  0.6 1.3 %collective-permute-start = (bf16[8,512,256]{2,1,0:T(8,128)(2,1)}, bf16[8,512,256]{2,1,0:T(8,128)(2,1)S(1)}, u32[]{:S(2)}, u32[]{:S(2)}) collective-permute-start(bf16[8,512,256]{2,1,0:T(8,128)(2,1)} %src_ref.3), channel_id=1, source_target_pairs={{1,0},{2,1},{3,2},{4,3},{5,4},{6,5},{7,6},{8,7},{9,8},{10,9},{11,1... | collective-permute-start | bytes 6291464 | tf_op jit(solution)/shard_map/ppermute | solution.py:220
  1.9 0.0 copy-start
  1.9 1.6 %copy-done = bf16[8,512,256]{2,1,0:T(8,128)(2,1)S(1)} copy-done((bf16[8,512,256]{2,1,0:T(8,128)(2,1)S(1)}, bf16[8,512,256]{2,1,0:T(8,128)(2,1)}, u32[]{:S(2)}) %copy-start) | copy-done | bytes 2097176
  3.5 0.0 copy-start.3
  3.5 0.7 %copy-done.3 = s32[2]{0:T(128)S(1)} copy-done((s32[2]{0:T(128)S(1)}, s32[2]{0:T(128)}, u32[]{:S(2)}) %copy-start.3) | copy-done | bytes 32
  4.2 15.0 %local_pairs.1 = (bf16[8,8,512,256]{3,2,1,0:T(8,128)(2,1)}, f32[9,8,256]{2,1,0:T(8,128)S(1)}, f32[8,512,256]{2,1,0:T(8,128)S(1)}, f32[8,512,256]{2,1,0:T(8,128)S...) custom-call(s32[2]{0:T(128)S(1)} %copy-done.3, bf16[8,512,256]{2,1,0:T(8,128)(2,1)S(1)} %copy-done), custom_call_target="tpu_custom_call" | custom-call | flops 5905580032 | bytes 11534336 | tf_op jit(solution)/shard_map/local_pairs/pallas_call | solution.py:243
  19.2 0.0 copy-start.1
  19.2 0.0 collective-permute-done.far_ref
  19.2 18.2 %far_pairs.1 = (bf16[8,8,512,256]{3,2,1,0:T(8,128)(2,1)}, f32[9,8,256]{2,1,0:T(8,128)S(1)}) custom-call(bf16[8,512,256]{2,1,0:T(8,128)(2,1)S(1)} %copy-done, bf16[8,512,256]{2,1,0:T(8,128)(2,1)S(1)} %collective-permute-done.far_ref, f32[8,512,256]{2,1,0:T(8,128)S(1)} %get-tuple-element.10.mu_ref, ...), custom_call_target="tpu_custom_call", output_to_operand_aliasing={{0}: (6, {})} | custom-call | flops 6979321856 | bytes 13631488 | tf_op jit(solution)/shard_map/far_pairs/pallas_call | solution.py:257
  37.5 0.0 copy-done.1
  37.5 0.0 copy-start.2
  37.5 0.6 %copy-done.2 = f32[9,8,256]{2,1,0:T(8,128)} copy-done((f32[9,8,256]{2,1,0:T(8,128)}, f32[9,8,256]{2,1,0:T(8,128)S(1)}, u32[]{:S(2)}) %copy-start.2) | copy-done | bytes 73752
  38.1 19.1 %share_totals.1 = f32[1,128]{1,0:T(1,128)} custom-call(f32[9,8,256]{2,1,0:T(8,128)} %copy-done.1, f32[9,8,256]{2,1,0:T(8,128)} %copy-done.2), custom_call_target="tpu_custom_call" | custom-call | tf_op jit(solution)/shard_map/share_totals/pallas_call | solution.py:268
  57.3 1.1 %slice_bitcast_fusion = f32[8]{0:T(128)} fusion(f32[1,128]{1,0:T(1,128)} %share_totals.1), kind=kLoop, calls=%fused_computation | loop fusion | bytes 64 | tf_op jit(solution)/shard_map/squeeze | solution.py:282
Async XLA Ops:
  0.6 18.6 %collective-permute-start = (bf16[8,512,256]{2,1,0:T(8,128)(2,1)}, bf16[8,512,256]{2,1,0:T(8,128)(2,1)S(1)}, u32[]{:S(2)}, u32[]{:S(2)}) collective-permute-start(bf16[8,512,256]{2,1,0:T(8,128)(2,1)} %src_ref.3), channel_id=1, source_target_pairs={{1,0},{2,1},{3,2},{4,3},{5,4},{6,5},{7,6},{8,7},{9,8},{10,9},{11,1... | collective-permute-start | bytes 6291464 | tf_op jit(solution)/shard_map/ppermute | solution.py:220
  1.9 1.6 %copy-start = (bf16[8,512,256]{2,1,0:T(8,128)(2,1)S(1)}, bf16[8,512,256]{2,1,0:T(8,128)(2,1)}, u32[]{:S(2)}) copy-start(bf16[8,512,256]{2,1,0:T(8,128)(2,1)} %src_ref.3) | copy-start | bytes 6291460
  3.5 0.7 %copy-start.3 = (s32[2]{0:T(128)S(1)}, s32[2]{0:T(128)}, u32[]{:S(2)}) copy-start(s32[2]{0:T(128)} %radius_ref.1) | copy-start | bytes 28
  19.2 18.3 %copy-start.1 = (f32[9,8,256]{2,1,0:T(8,128)}, f32[9,8,256]{2,1,0:T(8,128)S(1)}, u32[]{:S(2)}) copy-start(f32[9,8,256]{2,1,0:T(8,128)S(1)} %get-tuple-element.16.near_ref) | copy-start | bytes 221188
  37.5 0.6 %copy-start.2 = (f32[9,8,256]{2,1,0:T(8,128)}, f32[9,8,256]{2,1,0:T(8,128)S(1)}, u32[]{:S(2)}) copy-start(f32[9,8,256]{2,1,0:T(8,128)S(1)} %get-tuple-element.17.far_ref) | copy-start | bytes 221188

commit v3 on v1

v3 whole, which is shorter than its diff:
```python
import functools

import jax
import jax.numpy as jnp
from jax import lax
from jax.experimental import pallas as pl
from jax.experimental.pallas import tpu as pltpu
from jax.sharding import PartitionSpec as P

REACH = 8
MAX_RADIUS = 16
LANES = 128
ROWS = 176
BATCH = 2
LATE = 4
FIRST_LIMIT = 24 * 2**20
LAST_LIMIT = 18 * 2**20


def windows(tx):
    width = min(256, tx)
    out = []
    start = 0
    while start < tx:
        rows = min(ROWS, tx - start)
        middle = (start + rows // 2 - width // 2) // 16 * 16
        low = min(max(middle, 0), tx - width)
        assert low == 0 or low <= start - MAX_RADIUS
        assert low + width == tx or low + width >= start + rows + MAX_RADIUS
        out.append((start, rows, low))
        start += rows
    return width, out


def table(radius, shape, first, second, axis):
    i = lax.broadcasted_iota(jnp.int32, shape, 0) + first
    j = lax.broadcasted_iota(jnp.int32, shape, 1) + second
    diff = i - j
    sigma = radius.astype(jnp.float32) * 0.5
    dist = diff.astype(jnp.float32)
    value = jnp.exp(-(dist * dist) / (2.0 * sigma * sigma))
    value = jnp.where(jnp.abs(diff) <= radius, value, 0.0)
    return (value / jnp.sum(value, axis=axis, keepdims=True)).astype(jnp.bfloat16)


def blur_to(half_ref, gx_ref, blocks, width, slot, finish):
    for start, rows, low in blocks:
        acc = jnp.dot(
            gx_ref[start : start + rows, :],
            half_ref[slot, low : low + width, :],
            preferred_element_type=jnp.float32,
        )
        finish(start, rows, acc)


def fill_moments(src_ref, count, mu_ref, inv_ref, gx_ref, gy_ref, half_ref, blocks, width):
    def step(r, _):
        x = src_ref[r]
        half_ref[0] = jnp.dot(x, gy_ref[...], preferred_element_type=jnp.float32).astype(
            jnp.bfloat16
        )
        half_ref[1] = jnp.dot(x * x, gy_ref[...], preferred_element_type=jnp.float32).astype(
            jnp.bfloat16
        )
        for start, rows, low in blocks:
            gx = gx_ref[start : start + rows, :]
            mu = jnp.dot(
                gx, half_ref[0, low : low + width, :], preferred_element_type=jnp.float32
            )
            sq = jnp.dot(
                gx, half_ref[1, low : low + width, :], preferred_element_type=jnp.float32
            )
            mu_ref[r, start : start + rows, :] = mu
            inv_ref[r, start : start + rows, :] = lax.rsqrt(jnp.abs(sq - mu * mu + 0.1))
        return 0

    lax.fori_loop(0, count, step, 0)


def fill_pairs(
    runs, src_ref, far_ref, mu_a, inv_a, mu_b, inv_b, gx_ref, gy_ref,
    half_ref, stage, sems, sums_ref, ncc_ref, blocks, width, count, early=None, base=0,
):
    total = runs[-1][0] + runs[-1][4]
    steps = total // BATCH
    assert steps * BATCH == total and steps >= 2

    def decode(q):
        slot, place, s = jnp.int32(0), jnp.int32(0), jnp.int32(0)
        for first, run_slot, run_place, low, _ in runs:
            here = q >= first
            slot = jnp.where(here, run_slot, slot)
            place = jnp.where(here, run_place, place)
            s = jnp.where(here, low + q - first, s)
        return slot, s, place - s

    def copy(bank, b, s, d):
        return pltpu.make_async_copy(
            stage.at[bank * BATCH + b], ncc_ref.at[s, d - 1], sems.at[bank * BATCH + b]
        )

    def step(t, _):
        bank = lax.rem(t, 2)
        which = [decode(t * BATCH + b) for b in range(BATCH)]

        if early is None:

            @pl.when(t >= 2)
            def _():
                for b in range(BATCH):
                    copy(bank, b, 0, 1).wait()

        for b, (slot, s, d) in enumerate(which):
            half_ref[b] = jnp.dot(
                src_ref[s] * far_ref[slot], gy_ref[...], preferred_element_type=jnp.float32
            ).astype(jnp.bfloat16)
        for b, (slot, s, d) in enumerate(which):
            parts = []

            def finish(start, rows, acc):
                at = slice(start, start + rows)
                ncc = (acc - mu_a[s, at, :] * mu_b[slot, at, :]) * (
                    inv_a[s, at, :] * inv_b[slot, at, :]
                )
                if early is None:
                    stage[bank * BATCH + b, at, :] = ncc.astype(jnp.bfloat16)
                else:
                    early[base + t * BATCH + b, at, :] = ncc.astype(jnp.bfloat16)
                    parts.append(jnp.sum(ncc.reshape(rows // 8, 8, ncc.shape[1]), axis=0))

            blur_to(half_ref, gx_ref, blocks, width, b, finish)
            if early is None:
                copy(bank, b, s, d).start()
            else:
                sums_ref[jnp.where(d == 1, s, count)] = functools.reduce(jnp.add, parts)
        return 0

    lax.fori_loop(0, steps, step, 0)
    if early is not None:
        return
    for bank in range(2):
        for b in range(BATCH):
            copy(bank, b, 0, 1).wait()


def first_kernel(
    blocks, width, groups, count, devices, pixels,
    radius_ref, src_ref,
    early_ref, far_ref, mu_ref, inv_ref, gx_ref, gy_ref, out_ref,
    mu_far, inv_far, half_ref, sums_ref, mine, slots,
    halo_send, halo_recv, send_sems, recv_sems,
):
    me = lax.axis_index("gz")
    mesh_id = pl.DeviceIdType.MESH
    barrier = pltpu.get_barrier_semaphore()
    peers = [lax.rem(me + k, devices) for k in range(1, devices)]
    for peer in peers:
        pl.semaphore_signal(barrier, inc=1, device_id={"gz": peer}, device_id_type=mesh_id)
    for start, rows, low in blocks:
        gx_ref[start : start + rows, :] = table(radius_ref[0], (rows, width), start, low, 1)
    gy_ref[...] = table(radius_ref[1], gy_ref.shape, 0, 0, 0)
    pl.semaphore_wait(barrier, devices - 1)
    halo = [
        pltpu.make_async_remote_copy(
            src_ref=src_ref.at[j],
            dst_ref=far_ref.at[j],
            send_sem=halo_send.at[j],
            recv_sem=halo_recv.at[j],
            device_id={"gz": lax.rem(me + devices - 1, devices)},
            device_id_type=mesh_id,
        )
        for j in range(REACH)
    ]

    @pl.when(me > 0)
    def _():
        for copy in halo:
            copy.start()

    def arrive(a, b):
        @pl.when(me < devices - 1)
        def _():
            for j in range(a, b):
                halo[j].wait_recv()

        @pl.when(me == devices - 1)
        def _():
            for j in range(a, b):
                far_ref[j] = jnp.zeros(far_ref.shape[1:], far_ref.dtype)

    fill_moments(src_ref, count, mu_ref, inv_ref, gx_ref, gy_ref, half_ref, blocks, width)
    base, copies, running = 0, [], None
    for a, b, runs in groups:
        if b == 0:
            source, mu_b, inv_b = src_ref, mu_ref, inv_ref
        else:
            arrive(a, b)
            source, mu_b, inv_b = far_ref.at[pl.ds(a, b - a)], mu_far, inv_far
            fill_moments(
                source, b - a, mu_far, inv_far, gx_ref, gy_ref, half_ref, blocks, width
            )
        fill_pairs(
            runs, src_ref, source, mu_ref, inv_ref, mu_b, inv_b, gx_ref, gy_ref,
            half_ref, None, None, sums_ref, None, blocks, width, count, early_ref, base,
        )
        base += runs[-1][0] + runs[-1][4]
        if b == 1:
            sums = jnp.sum(jnp.sum(sums_ref[:count], axis=1), axis=1, keepdims=True)
            row = lax.broadcasted_iota(jnp.int32, (count, LANES), 0)
            lane = lax.broadcasted_iota(jnp.int32, (count, LANES), 1)
            spacing = 1.25 - jnp.broadcast_to(sums, (count, LANES)) / pixels
            mine[...] = jnp.broadcast_to(jnp.sum(spacing, axis=0, keepdims=True), mine.shape)
            running = jnp.sum(jnp.where(row <= lane, spacing, 0.0), axis=0, keepdims=True)
            for k, peer in enumerate(peers, 1):
                copy = pltpu.make_async_remote_copy(
                    src_ref=mine,
                    dst_ref=slots.at[k],
                    send_sem=send_sems.at[k],
                    recv_sem=recv_sems.at[k],
                    device_id={"gz": peer},
                    device_id_type=mesh_id,
                )
                copy.start()
                copies.append(copy)
    arrive(groups[-1][1], REACH)

    @pl.when(me > 0)
    def _():
        for copy in halo:
            copy.wait_send()

    for copy in copies:
        copy.wait()
    for k in range(1, devices):
        running = running + jnp.where(k <= me, slots[k, :1, :], 0.0)
    out_ref[...] = running * 0.015625


def last_kernel(
    blocks, width, groups, runs, begin, count,
    src_ref, far_ref, mu_ref, inv_ref, gx_ref, gy_ref, early_ref,
    ncc_ref,
    mu_far, inv_far, half_ref, stage, sems, early_sems,
):
    copies = []
    for _, _, done in groups:
        for _, _, place, low, number in done:
            for s in range(low, low + number):
                q = len(copies)
                copy = pltpu.make_async_copy(
                    early_ref.at[q], ncc_ref.at[s, place - s - 1], early_sems.at[q]
                )
                copy.start()
                copies.append(copy)
    source = far_ref.at[pl.ds(begin, REACH - begin)]
    fill_moments(
        source, REACH - begin, mu_far, inv_far, gx_ref, gy_ref, half_ref, blocks, width
    )
    fill_pairs(
        runs, src_ref, source, mu_ref, inv_ref, mu_far, inv_far, gx_ref, gy_ref,
        half_ref, stage, sems, None, ncc_ref, blocks, width, count,
    )
    for copy in copies:
        copy.wait()


def make_runs(places, count):
    out = []
    first = 0
    for slot, place in places:
        low, high = max(0, place - REACH), min(place, count)
        if high > low:
            out.append((first, slot, place, low, high - low))
            first += high - low
    return out


def per_device(sections, radius):
    count, tx, ty = sections.shape
    width, blocks = windows(tx)
    axis = lax.axis_size("gz")
    vmem = pl.BlockSpec(memory_space=pltpu.VMEM)
    smem = pl.BlockSpec(memory_space=pltpu.SMEM)
    hbm = pl.BlockSpec(memory_space=pl.ANY)
    shape = jax.ShapeDtypeStruct
    map_type = shape((count, tx, ty), jnp.float32)
    groups = [(0, 0, make_runs([(p, p) for p in range(count)], count))]
    for a, b in ((0, 1), (1, LATE)):
        groups.append((a, b, make_runs([(j - a, count + j) for j in range(a, b)], count)))
    late = make_runs([(j - LATE, count + j) for j in range(LATE, REACH)], count)
    pairs = sum(runs[-1][0] + runs[-1][4] for _, _, runs in groups)
    dma = pltpu.SemaphoreType.DMA
    early, far, mu, inv, gx, gy, positions = pl.pallas_call(
        functools.partial(first_kernel, blocks, width, groups, count, axis, tx * ty),
        out_shape=(
            shape((pairs, tx, ty), jnp.bfloat16),
            shape((REACH, tx, ty), jnp.bfloat16),
            map_type, map_type,
            shape((tx, width), jnp.bfloat16), shape((ty, ty), jnp.bfloat16),
            shape((1, LANES), jnp.float32),
        ),
        in_specs=[smem, vmem],
        out_specs=[vmem] * 7,
        scratch_shapes=[pltpu.VMEM((LATE - 1, tx, ty), jnp.float32)] * 2
        + [
            pltpu.VMEM((2, tx, ty), jnp.bfloat16),
            pltpu.VMEM((count + 1, 8, ty), jnp.float32),
            pltpu.VMEM((8, LANES), jnp.float32),
            pltpu.VMEM((axis, 8, LANES), jnp.float32),
            dma((REACH,)), dma((REACH,)), dma((axis,)), dma((axis,)),
        ],
        compiler_params=pltpu.CompilerParams(
            collective_id=0, has_side_effects=True, vmem_limit_bytes=FIRST_LIMIT
        ),
        name="first_pairs",
    )(radius, sections)
    ncc = pl.pallas_call(
        functools.partial(last_kernel, blocks, width, groups, late, LATE, count),
        out_shape=shape((count, REACH, tx, ty), jnp.bfloat16),
        in_specs=[vmem] * 6 + [hbm],
        out_specs=hbm,
        scratch_shapes=[pltpu.VMEM((REACH - LATE, tx, ty), jnp.float32)] * 2
        + [
            pltpu.VMEM((2, tx, ty), jnp.bfloat16),
            pltpu.VMEM((2 * BATCH, tx, ty), jnp.bfloat16),
            dma((2 * BATCH,)), dma((pairs,)),
        ],
        compiler_params=pltpu.CompilerParams(vmem_limit_bytes=LAST_LIMIT),
        name="last_pairs",
    )(sections, far, mu, inv, gx, gy, early)
    return (ncc, positions[0, :count])


def solution(mesh):
    in_specs = (P(("grp", "gz"), None, None), P())
    out_specs = (P(("grp", "gz"), None, None, None), P(("grp", "gz")))
    return jax.shard_map(
        per_device, mesh=mesh, in_specs=in_specs, out_specs=out_specs, check_vma=False
    )
```

time: 108 us -> 44.7 us (0.41)
  blocking collectives: 38.1 us -> 0 us
  local copies, waits for them, and re-layouts: 23.8 us -> 2.75 us
  Pallas kernels: 36.1 us -> 41.1 us
  other arithmetic: 4.91 us -> 0 us
  starting transfers between devices: 3.84 us -> 0 us
    unnamed x1 -> x0, blocking collectives: 38.1 us -> none
    unnamed x25 -> x4, local copies, waits for them, and re-layouts: 17.5 us -> 2.24 us
    slice x3 -> x0, local copies, waits for them, and re-layouts: 6.28 us -> none  [per_device(): sections[a:b]]
    pallas_call x4 -> x2, Pallas kernels: 36.1 us -> 41.1 us  [the longest x1 32.7 us: per_device(): pl.pallas_call(functools.partial(first_kernel, blocks, width, groups, cou...]
    ppermute x3 -> x0, starting transfers between devices: 3.84 us -> none  [per_device(): lax.ppermute(sections[a:b], 'gz', back)]
    reduce_sum x5 -> x0, other arithmetic: 3.72 us -> none  [the longest x1 1.38 us: per_device(): jnp.sum(spacing, keepdims=True)]
    mul x1 -> x0, other arithmetic: 1.19 us -> none  [per_device(): positions = (running + before) * 0.015625]
  transfers between devices with their start and end apart: 3 -> 0, of which waited for: 0 -> 0; matrix products, arithmetic and copies ran while one was open for 11% -> 0% of each run, Pallas kernels for 27% -> 0%
where the time goes in v3:
time: 44.7 us; the launch traced here: 44.5 us
  Pallas kernels  41.1 us (92%)
  local copies, waits for them, and re-layouts  2.75 us (6%)
  between operations  0.65 us (1%)
    pallas_call x1, Pallas kernels, per_device(): pl.pallas_call(functools.partial(first_kernel, blocks, width, groups, cou...  32.7 us
    pallas_call x1, Pallas kernels, per_device(): pl.pallas_call(functools.partial(last_kernel, blocks, width, groups, late...  8.39 us
    unnamed x4, local copies, waits for them, and re-layouts  2.24 us

profile of v3, /device:TPU:0, one launch (start us, length us, event | category | flops | bytes accessed | tf_op | source)
XLA Modules:
  0.0 44.5 jit_solution(13020025165453471679)
XLA Ops:
  0.6 0.0 copy-start
  0.6 1.6 %copy-done = bf16[8,512,256]{2,1,0:T(8,128)(2,1)S(1)} copy-done((bf16[8,512,256]{2,1,0:T(8,128)(2,1)S(1)}, bf16[8,512,256]{2,1,0:T(8,128)(2,1)}, u32[]{:S(2)}) %copy-start) | copy-done | bytes 2097176
  2.2 0.0 copy-start.1
  2.2 0.7 %copy-done.1 = s32[2]{0:T(128)S(1)} copy-done((s32[2]{0:T(128)S(1)}, s32[2]{0:T(128)}, u32[]{:S(2)}) %copy-start.1) | copy-done | bytes 32
  2.9 32.7 %first_pairs.1 = (bf16[54,512,256]{2,1,0:T(8,128)(2,1)S(1)}, bf16[8,512,256]{2,1,0:T(8,128)(2,1)S(1)}, f32[8,512,256]{2,1,0:T(8,128)S(1)}, f32[8,512,256]{2,1,0:...) custom-call(s32[2]{0:T(128)S(1)} %copy-done.1, ...), custom_call_target="tpu_custom_call" | custom-call | tf_op jit(solution)/shard_map/first_pairs/pallas_call | solution.py:293
  35.6 8.4 %last_pairs.1 = bf16[8,8,512,256]{3,2,1,0:T(8,128)(2,1)} custom-call(bf16[8,512,256]{2,1,0:T(8,128)(2,1)S(1)} %copy-done, bf16[8,512,256]{2,1,0:T(8,128)(2,1)S(1)} %get-tuple-element.9.far_ref, f32[8,512,256]{2,1,0:T(8,128)S(1)} %get-tuple-element.10.mu_ref, f32[8,512,256]{2,1,0:T(8,128)S(1)} %get-tuple-element.11.inv_ref, ...), custom_call_target="tpu_custom_call" | custom-call | tf_op jit(solution)/shard_map/last_pairs/pallas_call | solution.py:317
  44.0 0.5 %slice_bitcast_fusion = f32[8]{0:T(128)} fusion(f32[1,128]{1,0:T(1,128)S(1)} %get-tuple-element.15), kind=kLoop, calls=%fused_computation | loop fusion | bytes 64 | tf_op jit(solution)/shard_map/squeeze | solution.py:331
Async XLA Ops:
  0.6 1.6 %copy-start = (bf16[8,512,256]{2,1,0:T(8,128)(2,1)S(1)}, bf16[8,512,256]{2,1,0:T(8,128)(2,1)}, u32[]{:S(2)}) copy-start(bf16[8,512,256]{2,1,0:T(8,128)(2,1)} %src_ref.3) | copy-start | bytes 6291460
  2.2 0.7 %copy-start.1 = (s32[2]{0:T(128)S(1)}, s32[2]{0:T(128)}, u32[]{:S(2)}) copy-start(s32[2]{0:T(128)} %radius_ref.1) | copy-start | bytes 28

commit v4 on v3

--- a/solution.py
+++ b/solution.py
@@ -53,7 +53,7 @@
         finish(start, rows, acc)
 
 
-def fill_moments(src_ref, count, mu_ref, inv_ref, gx_ref, gy_ref, half_ref, blocks, width):
+def fill_moments(src_ref, count, mu_ref, inv_ref, gx_ref, gy_ref, half_ref, blocks, width, begin=0):
     def step(r, _):
         x = src_ref[r]
         half_ref[0] = jnp.dot(x, gy_ref[...], preferred_element_type=jnp.float32).astype(
@@ -74,7 +74,7 @@
             inv_ref[r, start : start + rows, :] = lax.rsqrt(jnp.abs(sq - mu * mu + 0.1))
         return 0
 
-    lax.fori_loop(0, count, step, 0)
+    lax.fori_loop(begin, count, step, 0)
 
 
 def fill_pairs(
@@ -159,6 +159,8 @@
     for start, rows, low in blocks:
         gx_ref[start : start + rows, :] = table(radius_ref[0], (rows, width), start, low, 1)
     gy_ref[...] = table(radius_ref[1], gy_ref.shape, 0, 0, 0)
+    half = count // 2
+    fill_moments(src_ref, half, mu_ref, inv_ref, gx_ref, gy_ref, half_ref, blocks, width)
     pl.semaphore_wait(barrier, devices - 1)
     halo = [
         pltpu.make_async_remote_copy(
@@ -188,7 +190,7 @@
             for j in range(a, b):
                 far_ref[j] = jnp.zeros(far_ref.shape[1:], far_ref.dtype)
 
-    fill_moments(src_ref, count, mu_ref, inv_ref, gx_ref, gy_ref, half_ref, blocks, width)
+    fill_moments(src_ref, count, mu_ref, inv_ref, gx_ref, gy_ref, half_ref, blocks, width, half)
     base, copies, running = 0, [], None
     for a, b, runs in groups:
         if b == 0:

time: 44.7 us -> 45.4 us (1.016)
  Pallas kernels: 41.1 us -> 41.8 us
    pallas_call x1, Pallas kernels: 32.7 us -> 33.4 us  [per_device(): pl.pallas_call(functools.partial(first_kernel, blocks, width, groups, cou...]
where the time goes in v4:
time: 45.4 us; the launch traced here: 45.2 us
  Pallas kernels  41.8 us (92%)
  local copies, waits for them, and re-layouts  2.75 us (6%)
  between operations  0.65 us (1%)
    pallas_call x1, Pallas kernels, per_device(): pl.pallas_call(functools.partial(first_kernel, blocks, width, groups, cou...  33.4 us
    pallas_call x1, Pallas kernels, per_device(): pl.pallas_call(functools.partial(last_kernel, blocks, width, groups, late...  8.39 us
    unnamed x4, local copies, waits for them, and re-layouts  2.24 us

profile of v4, /device:TPU:0, one launch (start us, length us, event | category | flops | bytes accessed | tf_op | source)
XLA Modules:
  0.0 45.2 jit_solution(15299144893533944590)
XLA Ops:
  0.6 0.0 copy-start
  0.6 1.6 %copy-done = bf16[8,512,256]{2,1,0:T(8,128)(2,1)S(1)} copy-done((bf16[8,512,256]{2,1,0:T(8,128)(2,1)S(1)}, bf16[8,512,256]{2,1,0:T(8,128)(2,1)}, u32[]{:S(2)}) %copy-start) | copy-done | bytes 2097176
  2.2 0.0 copy-start.1
  2.2 0.7 %copy-done.1 = s32[2]{0:T(128)S(1)} copy-done((s32[2]{0:T(128)S(1)}, s32[2]{0:T(128)}, u32[]{:S(2)}) %copy-start.1) | copy-done | bytes 32
  2.9 33.4 %first_pairs.1 = (bf16[54,512,256]{2,1,0:T(8,128)(2,1)S(1)}, bf16[8,512,256]{2,1,0:T(8,128)(2,1)S(1)}, f32[8,512,256]{2,1,0:T(8,128)S(1)}, f32[8,512,256]{2,1,0:...) custom-call(s32[2]{0:T(128)S(1)} %copy-done.1, ...), custom_call_target="tpu_custom_call" | custom-call | tf_op jit(solution)/shard_map/first_pairs/pallas_call | solution.py:295
  36.3 8.4 %last_pairs.1 = bf16[8,8,512,256]{3,2,1,0:T(8,128)(2,1)} custom-call(bf16[8,512,256]{2,1,0:T(8,128)(2,1)S(1)} %copy-done, bf16[8,512,256]{2,1,0:T(8,128)(2,1)S(1)} %get-tuple-element.9.far_ref, f32[8,512,256]{2,1,0:T(8,128)S(1)} %get-tuple-element.10.mu_ref, f32[8,512,256]{2,1,0:T(8,128)S(1)} %get-tuple-element.11.inv_ref, ...), custom_call_target="tpu_custom_call" | custom-call | tf_op jit(solution)/shard_map/last_pairs/pallas_call | solution.py:319
  44.7 0.5 %slice_bitcast_fusion = f32[8]{0:T(128)} fusion(f32[1,128]{1,0:T(1,128)S(1)} %get-tuple-element.15), kind=kLoop, calls=%fused_computation | loop fusion | bytes 64 | tf_op jit(solution)/shard_map/squeeze | solution.py:333
Async XLA Ops:
  0.6 1.6 %copy-start = (bf16[8,512,256]{2,1,0:T(8,128)(2,1)S(1)}, bf16[8,512,256]{2,1,0:T(8,128)(2,1)}, u32[]{:S(2)}) copy-start(bf16[8,512,256]{2,1,0:T(8,128)(2,1)} %src_ref.3) | copy-start | bytes 6291460
  2.2 0.7 %copy-start.1 = (s32[2]{0:T(128)S(1)}, s32[2]{0:T(128)}, u32[]{:S(2)}) copy-start(s32[2]{0:T(128)} %radius_ref.1) | copy-start | bytes 28
